TPU v7x, 512 devices: a whole 4x4x16 slice. The times are simulated.
512 devices in a mesh: wide: 32 (over y, x, core), narrow: 16 (over z).
Axes of the slice: x: 4, y: 4, z: 16, core: 2. Of those that a mesh axis runs over, the one named last changes fastest.
Arguments:
- factors: bfloat16 [32, 8192, 512], P('narrow', 'wide'), may hold values from -0.41992188 to 0.41992188
- pairs: int32 [256, 2], replicated, may hold values from 0 to 31, as said below
Outputs:
- exchange: float32 [8192, 8192], P(('wide', 'narrow'))
Inputs may be any that keep to these rules, and one draw needn't show every extreme that they name: Rows are sorted by row block; each row block has 1 to 15 pairs and some row block exactly 15; column blocks within one row block are distinct.
All inputs are finite; a program needn't handle non-finite values.
Results may differ from a plain program's by a relative error of at most 0.0003.
Values may be sent and summed in bfloat16 or wider, within the bound.
A program may use at most 128 MiB of HBM per device.

v0:
```python
import jax
import jax.numpy as jnp
from jax import lax
from jax.sharding import PartitionSpec as P


def shards(factors, pairs):
    nwide = lax.axis_size("wide")
    nnarrow = lax.axis_size("narrow")
    myblock = lax.axis_index("wide")
    rows = factors.shape[1]
    maxslots = 2 * (nwide // 4) - 1
    is_mine = (pairs[:, 0] == myblock).astype(jnp.int32)
    ranked = jnp.cumsum(is_mine) - 1
    onehot = (is_mine[:, None] == 1) & (ranked[:, None] == jnp.arange(maxslots)[None, :])
    slot_live = jnp.any(onehot, axis=0)
    slot_col = jnp.sum(jnp.where(onehot, pairs[:, 1:2], 0), axis=0)
    product = lax.dot_general(
        factors,
        lax.all_gather(factors, "wide", axis=1, tiled=True),
        (((0, 2), (0, 2)), ((), ())),
        preferred_element_type=jnp.float32,
    )
    by_block = product.reshape(rows, nwide, rows)
    tiles = jnp.take(by_block, slot_col, axis=1)
    tiles = jnp.where(slot_live[None, :, None], tiles, 0.0)
    summed = lax.psum_scatter(tiles, "narrow", scatter_dimension=0, tiled=True)
    placed = jnp.zeros((rows // nnarrow, nwide, rows), jnp.float32)
    placed = placed.at[:, slot_col, :].add(summed)
    return placed.reshape(rows // nnarrow, nwide * rows)


def solution(mesh):
    placed = (P("narrow", "wide", None), P())
    return jax.shard_map(
        shards, mesh=mesh, in_specs=placed, out_specs=P(("wide", "narrow"), None), check_vma=False
    )
```

profile of v0, /device:TPU:12, one launch (start us, length us, event | category | flops | bytes accessed | tf_op | source)
XLA Modules:
  0.0 223.7 jit_solution(14599575604912654026)
XLA Ops:
  6.5 0.0 all-gather.2.cloned.1.call-start
  6.5 0.7 all-gather.2.cloned.1.call-update
  7.3 0.0 reduce-scatter.2.cloned.1.call-start
  7.3 0.7 slice.16
  8.0 0.7 compare_reduce_fusion
  8.7 0.3 reduce-window.9
  9.0 0.1 slice.14
  9.1 0.1 slice_reduce_fusion
  9.2 0.1 add_bitcast_fusion
  9.3 0.1 select_reduce_fusion
  9.4 0.1 fusion.1
  9.6 91.7 %all-gather.2.cloned.1.call-done = bf16[2,8192,512]{2,1,0:T(8,128)(2,1)} async-done(((bf16[2,256,512]{2,1,0:T(8,128)(2,1)}), bf16[2,8192,512]{2,1,0:T(8,128)(2,1)}) %all-gather.2.cloned.1.call-update) | async-done | bytes 16777232 | tf_op jit(solution)/shard_map/all_gather | solution.py:20
  101.3 13.7 %fusion.3 = f32[256,8192,1]{1,0,2:T(8,128)} fusion(bf16[2,256,512]{2,1,0:T(8,128)(2,1)} %param.2, bf16[2,8192,512]{2,1,0:T(8,128)(2,1)} %all-gather.2.cloned.1.call-done), kind=kOutput, calls=%fused_computation.17 | convolution fusion | flops 4294967296 | bytes 25690112 | tf_op jit(solution)/shard_map/dot_general | solution.py:18
  115.0 7.7 %copy.10 = f32[32,32,8,256]{3,2,0,1:T(8,128)} copy(f32[32,32,8,256]{3,2,1,0:T(8,128)} %bitcast.20) | data formatting | bytes 16777216 | tf_op jit(solution)/shard_map/reshape | solution.py:24
  122.7 6.1 %gather_fusion = f32[15,256,256]{2,1,0:T(8,128)} fusion(f32[256,32,256]{2,0,1:T(8,128)} %bitcast.21, s32[1024]{0:T(1024)S(1)} %pad_clamp_fusion), kind=kCustom, calls=%fused_computation | custom fusion | bytes 7864380 | tf_op jit(solution)/shard_map/jit(_take)/gather | solution.py:25
  128.8 4.6 %select_bitcast_fusion = f32[256,15,256]{2,0,1:T(8,128)} fusion(f32[15,256,256]{2,1,0:T(8,128)} %gather_fusion, pred[15]{0:T(512)(128)(4,1)S(1)} %fusion.1, pred[15]{0:T(512)(128)(4,1)S(1)} %compare_and_fusion), kind=kLoop, calls=%fused_computation.3 | loop fusion | flops 1966080 | bytes 7864350 | tf_op jit(solution)/shard_map/jit(_where)/select_n | solution.py:26
  133.4 0.0 reduce-scatter.2.cloned.1.call-update
  133.4 80.6 %reduce-scatter.2.cloned.1.call-done = f32[16,15,256]{2,0,1:T(8,128)} async-done(((f32[256,15,256]{2,0,1:T(8,128)}), f32[16,15,256]{2,0,1:T(8,128)}) %reduce-scatter.2.cloned.1.call-update) | async-done | bytes 245776 | tf_op jit(solution)/shard_map/reduce_scatter | solution.py:27
  214.1 1.9 scatter_fusion
  216.0 0.8 copy.8
  (5 shorter events, 0.1 us)
Async XLA Ops:
  6.5 94.7 %all-gather.2.cloned.1.call-start = ((), (), s32[]{:S(2)}) async-start(), calls=%async_computation.1 | async-start | bytes 17301504 | tf_op jit(solution)/shard_map/all_gather | solution.py:20
  7.3 206.8 %reduce-scatter.2.cloned.1.call-start = ((), (), s32[]{:S(2)}) async-start(), calls=%async_computation.2 | async-start | bytes 4177920 | tf_op jit(solution)/shard_map/reduce_scatter | solution.py:27
Sparse Core Ops, SparseCore 0:
  10.5 90.6 all-gather.1
  133.5 80.4 reduce-scatter.1
where the time goes:
time: 224 us
  waiting for transfers between devices  173 us (77%)
  local copies, waits for them, and re-layouts  15.6 us (7%)
  matrix products  13.7 us (6%)
  between operations  13.4 us (6%)
  other arithmetic  7.92 us (4%)
    all_gather x1, waiting for transfers between devices, shards(): lax.all_gather(factors, 'wide', axis=1, tiled=True)  91.7 us
    reduce_scatter x1, waiting for transfers between devices, shards(): summed = lax.psum_scatter(tiles, 'narrow', scatter_dimension=0, tiled=True)  80.6 us
    dot_general x1, matrix products, shards(): lax.dot_general(factors, lax.all_gather(factors, 'wide', axis=1, tiled=Tr...  13.7 us
    reshape x1, local copies, waits for them, and re-layouts, shards(): by_block = product.reshape(rows, nwide, rows)  7.72 us
    gather x1, local copies, waits for them, and re-layouts, shards(): tiles = jnp.take(by_block, slot_col, axis=1)  6.08 us
    select_n x1, other arithmetic, shards(): tiles = jnp.where(slot_live[None, :, None], tiles, 0.0)  4.61 us
  transfers between devices with their start and end apart: 2, of which 2 were waited for; matrix products, arithmetic and copies ran while one was open for 1% of the time, Pallas kernels for 0%

commit v1 on v0

v1 whole, which is shorter than its diff:
```python
import functools

import jax
import jax.numpy as jnp
from jax import lax
from jax.experimental import pallas as pl
from jax.experimental.pallas import tpu as pltpu
from jax.sharding import PartitionSpec as P

MESH = pl.DeviceIdType.MESH
NX = NY = 4
SLOTS = 16
STEP = 16.0
TOP = 32000.0


def place():
    w = lax.axis_index("wide")
    return w // (2 * NX), lax.rem(w // 2, NX), lax.rem(w, 2)


def wide(y, x, q):
    return {"wide": (y * NX + x) * 2 + q}


def item(axis, distance, other):
    if distance == 0:
        return other
    return (0 if axis == "x" else 2 * NX - 2) + 2 * distance + other


def cross_gather(buf, halves, axes, send, recv):
    y, x, q = place()
    near = {
        ("x", 1): wide(y, lax.rem(x + 1, NX), q),
        ("x", -1): wide(y, lax.rem(x + NX - 1, NX), q),
        ("y", 1): wide(lax.rem(y + 1, NY), x, q),
        ("y", -1): wide(lax.rem(y + NY - 1, NY), x, q),
        "core": wide(y, x, 1 - q),
    }
    started = []

    def copy(src, dst, half, to):
        c = pltpu.make_async_remote_copy(
            src_ref=buf.at[(src,) + halves[half]],
            dst_ref=buf.at[(dst,) + halves[half]],
            send_sem=send.at[len(started)],
            recv_sem=recv.at[dst, half],
            device_id=near[to],
            device_id_type=MESH,
        )
        c.start()
        started.append(c)

    def arrived(dst, half):
        pltpu.make_async_remote_copy(
            src_ref=buf.at[(dst,) + halves[half]],
            dst_ref=buf.at[(dst,) + halves[half]],
            send_sem=send.at[0],
            recv_sem=recv.at[dst, half],
            device_id=near["core"],
            device_id_type=MESH,
        ).wait_recv()

    for first in (0, 1):
        for a in axes:
            copy(0, item(a, 3, 0), first, (a, 1))
            copy(0, item(a, 1, 0), 1 - first, (a, -1))
    for half in (0, 1):
        copy(0, 1, half, "core")
    for a in axes:
        arrived(item(a, 3, 0), 0)
        copy(item(a, 3, 0), item(a, 2, 0), 0, (a, 1))
        arrived(item(a, 1, 0), 1)
        copy(item(a, 1, 0), item(a, 2, 0), 1, (a, -1))
    for a in axes:
        copy(item(a, 3, 0), item(a, 3, 1), 0, "core")
        copy(item(a, 1, 0), item(a, 1, 1), 1, "core")
    for a in axes:
        arrived(item(a, 3, 0), 1)
        copy(item(a, 3, 0), item(a, 3, 1), 1, "core")
        arrived(item(a, 1, 0), 0)
        copy(item(a, 1, 0), item(a, 1, 1), 0, "core")
    for a in axes:
        for half in (0, 1):
            arrived(item(a, 2, 0), half)
            copy(item(a, 2, 0), item(a, 2, 1), half, "core")
    for half in (0, 1):
        arrived(1, half)
        for a in axes:
            for d in (1, 2, 3):
                arrived(item(a, d, 1), half)
    for c in started:
        c.wait_send()


def encode(out, value):
    slots = value.shape[0]
    most = jnp.maximum(jnp.max(jnp.abs(value), axis=1), 1e-30)
    level = jnp.ceil(jnp.log2(most) * STEP)
    out[slots] = level.astype(jnp.int32).astype(jnp.int16)
    inverse = jnp.exp2(level * (-1.0 / STEP)) * TOP
    out[:slots] = jnp.round(value * inverse[:, None, :]).astype(jnp.int32).astype(jnp.int16)


def scales(code):
    return jnp.exp2(code.astype(jnp.int32).astype(jnp.float32) * (1.0 / STEP)) * (1.0 / TOP)


def decode(ref):
    slots = ref.shape[0] - 1
    scale = scales(ref[slots])
    return ref[:slots].astype(jnp.int32).astype(jnp.float32) * scale[:, None, :]


def kernel(
    nz, table, factors, out, blocks, partial, right_out, right_in, left_out, left_in, parts, scale,
    local, gsend, grecv, rsend, rrecv, lsend, lrecv, xsend, xrecv,
):
    y, x, q = place()
    z = lax.axis_index("narrow")
    rows = blocks.shape[2]
    chunk = rows // nz
    slots = partial.shape[0]
    up, down = lax.rem(z + 1, nz), lax.rem(z + nz - 1, nz)

    own = pltpu.make_async_copy(factors, blocks.at[0], local)
    own.start()
    barrier = pltpu.get_barrier_semaphore()
    for peer in (
        wide(y, lax.rem(x + 1, NX), q),
        wide(y, lax.rem(x + NX - 1, NX), q),
        wide(lax.rem(y + 1, NY), x, q),
        wide(lax.rem(y + NY - 1, NY), x, q),
        wide(y, x, 1 - q),
        {"narrow": up},
        {"narrow": down},
    ):
        pl.semaphore_signal(barrier, inc=1, device_id=peer, device_id_type=MESH)
    own.wait()
    pl.semaphore_wait(barrier, 7)

    cross_gather(blocks, ((0,), (1,)), ("x", "y"), gsend, grecv)

    def one(s, _):
        i, j = table[s], table[slots + s]
        contract = (((1,), (1,)), ((), ()))
        partial[s] = lax.dot_general(
            blocks[i, 0], blocks[j, 0], contract, preferred_element_type=jnp.float32
        ) + lax.dot_general(blocks[i, 1], blocks[j, 1], contract, preferred_element_type=jnp.float32)
        return 0

    lax.fori_loop(0, slots, one, 0)

    def mine(dest):
        return partial[:, pl.ds(pl.multiple_of(dest * chunk, chunk), chunk), :]

    def hop(src, dst, sends, recvs, t, to):
        return pltpu.make_async_remote_copy(
            src_ref=src.at[t],
            dst_ref=dst.at[t],
            send_sem=sends.at[t],
            recv_sem=recvs.at[t],
            device_id={"narrow": to},
            device_id_type=MESH,
        )

    nright, nleft = nz // 2, nz // 2 - 1
    rights = [hop(right_out, right_in, rsend, rrecv, t, up) for t in range(nright)]
    lefts = [hop(left_out, left_in, lsend, lrecv, t, down) for t in range(nleft)]
    for t in range(nright):
        value = mine(lax.rem(z + nz // 2 - t, nz))
        if t:
            rights[t - 1].wait_recv()
            value += decode(right_in.at[t - 1])
        encode(right_out.at[t], value)
        rights[t].start()
        if t < nleft:
            value = mine(lax.rem(z + nz - nleft + t, nz))
            if t:
                lefts[t - 1].wait_recv()
                value += decode(left_in.at[t - 1])
            encode(left_out.at[t], value)
            lefts[t].start()
    value = mine(z)
    lefts[-1].wait_recv()
    value += decode(left_in.at[nleft - 1])
    rights[-1].wait_recv()
    value += decode(right_in.at[nright - 1])
    encode(parts.at[0], value)

    cut = slots // 2
    cross_gather(parts, ((pl.ds(0, cut),), (pl.ds(cut, slots + 1 - cut),)), ("x",), xsend, xrecv)
    for k in range(parts.shape[0]):
        scale[k] = scales(parts[k, slots])
    nblk = out.shape[1] // rows
    for c in range(nblk):
        base = 2 * slots + 3 * c
        src, slot, live = table[base], table[base + 1], table[base + 2]
        tile = parts[src, slot].astype(jnp.int32).astype(jnp.float32) * scale[src, pl.ds(slot, 1), :]
        out[:, c * rows : (c + 1) * rows] = jnp.where(live > 0, tile, 0.0)
    for c in rights + lefts:
        c.wait_send()


def tables(pairs, turn):
    y, x, q = place()
    r, c = pairs[:, 0], pairs[:, 1]
    nblk = 2 * NX * NY
    node = (r // (2 * NX)) * NX + lax.rem(c // 2, NX)
    hot = (node[:, None] == jnp.arange(NX * NY)[None, :]).astype(jnp.int32)
    rank = jnp.sum((jnp.cumsum(hot, axis=0) - hot) * hot, axis=1)
    core, slot = lax.rem(rank, 2), rank // 2 - turn * SLOTS
    inside = (slot >= 0) & (slot < SLOTS)
    here = (node == y * NX + x) & (core == q) & inside
    pick = here[:, None] & (slot[:, None] == jnp.arange(SLOTS)[None, :])
    d = lax.rem(lax.rem(r // 2, NX) - x + NX, NX)
    row = 2 * d + (lax.rem(r, 2) ^ q)
    e = lax.rem(c // (2 * NX) - y + NY, NY)
    col = jnp.where(e == 0, 0, 2 * NX - 2 + 2 * e) + (lax.rem(c, 2) ^ q)
    row = jnp.sum(jnp.where(pick, row[:, None], 0), axis=0)
    col = jnp.sum(jnp.where(pick, col[:, None], 0), axis=0)
    want = (r == (y * NX + x) * 2 + q) & inside
    listed = want[:, None] & (c[:, None] == jnp.arange(nblk)[None, :])
    src = 2 * lax.rem(lax.rem(c // 2, NX) - x + NX, NX) + (core ^ q)
    found = [jnp.sum(jnp.where(listed, v[:, None], 0), axis=0) for v in (src, slot, jnp.ones_like(src))]
    return jnp.concatenate([row, col, jnp.stack(found, axis=1).reshape(-1)]), jnp.max(jnp.sum(hot, axis=0))


def shards(factors, pairs):
    nz = lax.axis_size("narrow")
    two, rows, occ = factors.shape
    nblk = lax.axis_size("wide")
    chunk = rows // nz
    nright, nleft = nz // 2, nz // 2 - 1
    code = (SLOTS + 1, chunk, rows)
    items = 2 * (NX + NY - 1)

    def run(table):
        return pl.pallas_call(
            functools.partial(kernel, nz),
            out_shape=jax.ShapeDtypeStruct((chunk, nblk * rows), jnp.float32),
            in_specs=[pl.BlockSpec(memory_space=pltpu.SMEM), pl.BlockSpec(memory_space=pl.ANY)],
            out_specs=pl.BlockSpec(memory_space=pltpu.VMEM),
            scratch_shapes=[
                pltpu.VMEM((items, two, rows, occ), jnp.bfloat16),
                pltpu.VMEM((SLOTS, rows, rows), jnp.float32),
                pltpu.VMEM((nright,) + code, jnp.int16),
                pltpu.VMEM((nright,) + code, jnp.int16),
                pltpu.VMEM((nleft,) + code, jnp.int16),
                pltpu.VMEM((nleft,) + code, jnp.int16),
                pltpu.VMEM((2 * NX,) + code, jnp.int16),
                pltpu.VMEM((2 * NX, SLOTS, rows), jnp.float32),
                pltpu.SemaphoreType.DMA,
                pltpu.SemaphoreType.DMA((26,)),
                pltpu.SemaphoreType.DMA((items, 2)),
                pltpu.SemaphoreType.DMA((nright,)),
                pltpu.SemaphoreType.DMA((nright,)),
                pltpu.SemaphoreType.DMA((nleft,)),
                pltpu.SemaphoreType.DMA((nleft,)),
                pltpu.SemaphoreType.DMA((14,)),
                pltpu.SemaphoreType.DMA((2 * NX, 2)),
            ],
            compiler_params=pltpu.CompilerParams(
                collective_id=0, has_side_effects=True, vmem_limit_bytes=48 * 1024 * 1024
            ),
        )(table, factors)

    table, most = tables(pairs, 0)
    out = run(table)
    return lax.cond(most > 2 * SLOTS, lambda o: o + run(tables(pairs, 1)[0]), lambda o: o, out)


def solution(mesh):
    placed = (P("narrow", "wide", None), P())
    return jax.shard_map(
        shards, mesh=mesh, in_specs=placed, out_specs=P(("wide", "narrow"), None), check_vma=False
    )
```

time: 224 us -> 95.5 us (0.43)
  the two profiles are of different devices: /device:TPU:12 before, /device:TPU:1 now
where the time goes in v1:
time: 95.5 us; the launch traced here: 95.3 us
  Pallas kernels  90.8 us (95%)
  other arithmetic  1.88 us (2%)
  local copies, waits for them, and re-layouts  1.87 us (2%)
    pallas_call x1, Pallas kernels, run(): pl.pallas_call(functools.partial(kernel, nz), out_shape=jax.ShapeDtypeStr...  90.8 us

profile of v1, /device:TPU:1, one launch (start us, length us, event | category | flops | bytes accessed | tf_op | source)
XLA Modules:
  0.0 95.3 jit_solution(10541380582106516120)
XLA Ops:
  0.0 0.0 copy-start.1
  0.0 0.7 copy-done.1
  0.7 0.6 reduce-window.14
  1.3 0.2 slice_reduce_fusion.1
  1.6 0.1 fusion.21
  1.7 0.6 reduce_max.9
  3.1 0.1 select_reduce_fusion.9
  3.2 0.2 select_reduce_fusion.7
  3.4 0.1 copy.14
  3.4 0.1 reshape.190
  3.6 0.1 pad_add_fusion.3.table
  3.6 0.0 copy-start
  3.6 90.8 %shard_map.30 = f32[16,8192]{1,0:T(8,128)S(1)} custom-call(s32[128]{0:T(128)S(1)} %pad_add_fusion.3.table, bf16[2,256,512]{2,1,0:T(8,128)(2,1)} %factors.1), custom_call_target="tpu_custom_call" | custom-call | tf_op jit(solution)/shard_map/pallas_call | solution.py:240
  94.5 0.0 copy-done
  94.5 0.8 copy.22
  (10 shorter events, 0.2 us)
Async XLA Ops:
  0.0 0.7 copy-start.1
  3.6 90.9 %copy-start = (bf16[2,256,512]{2,1,0:T(8,128)(2,1)S(1)}, bf16[2,256,512]{2,1,0:T(8,128)(2,1)}, u32[]{:S(2)}) copy-start(bf16[2,256,512]{2,1,0:T(8,128)(2,1)} %factors.1) | copy-start | bytes 1572868

commit v2 on v0

v2 whole, which is shorter than its diff:
```python
import functools

import jax
import jax.numpy as jnp
from jax import lax
from jax.experimental import pallas as pl
from jax.experimental.pallas import tpu as pltpu
from jax.sharding import PartitionSpec as P

MESH = pl.DeviceIdType.MESH
NX = NY = 4
NODES = NX * NY
STREAMS = (3, 3, 3)
SLOTS = sum(STREAMS)
LANES = 128
STEP = 16.0
TOP = 32000.0
PATTERN = "skip"
BALANCE, FIXES = 4, 6


def place():
    w = lax.axis_index("wide")
    return w // (2 * NX), lax.rem(w // 2, NX), lax.rem(w, 2)


def wide(y, x, q):
    return {"wide": (y * NX + x) * 2 + q}


def item(axis, distance, other):
    if distance == 0:
        return other
    return (0 if axis == "x" else 2 * NX - 2) + 2 * distance + other


ITEMS = 2 * (NX + NY - 1)


def neighbours():
    y, x, q = place()
    return {
        ("x", 1): wide(y, lax.rem(x + 1, NX), q),
        ("x", -1): wide(y, lax.rem(x + NX - 1, NX), q),
        ("y", 1): wide(lax.rem(y + 1, NY), x, q),
        ("y", -1): wide(lax.rem(y + NY - 1, NY), x, q),
        "core": wide(y, x, 1 - q),
    }


def cross_gather(buf, halves, send, recv):
    near = neighbours()
    started = []

    def copy(src, dst, half, to):
        c = pltpu.make_async_remote_copy(
            src_ref=buf.at[(src,) + halves[half]],
            dst_ref=buf.at[(dst,) + halves[half]],
            send_sem=send.at[len(started)],
            recv_sem=recv.at[dst, half],
            device_id=near[to],
            device_id_type=MESH,
        )
        c.start()
        started.append(c)

    def arrived(dst, half):
        pltpu.make_async_remote_copy(
            src_ref=buf.at[(dst,) + halves[half]],
            dst_ref=buf.at[(dst,) + halves[half]],
            send_sem=send.at[0],
            recv_sem=recv.at[dst, half],
            device_id=near["core"],
            device_id_type=MESH,
        ).wait_recv()

    def start():
        for first in (0, 1):
            for a in "xy":
                copy(0, item(a, 3, 0), first, (a, 1))
                copy(0, item(a, 1, 0), 1 - first, (a, -1))
        for half in (0, 1):
            copy(0, 1, half, "core")

    def relay():
        for a in "xy":
            arrived(item(a, 3, 0), 0)
            copy(item(a, 3, 0), item(a, 2, 0), 0, (a, 1))
            arrived(item(a, 1, 0), 1)
            copy(item(a, 1, 0), item(a, 2, 0), 1, (a, -1))
        for a in "xy":
            copy(item(a, 3, 0), item(a, 3, 1), 0, "core")
            copy(item(a, 1, 0), item(a, 1, 1), 1, "core")
        for a in "xy":
            arrived(item(a, 3, 0), 1)
            copy(item(a, 3, 0), item(a, 3, 1), 1, "core")
            arrived(item(a, 1, 0), 0)
            copy(item(a, 1, 0), item(a, 1, 1), 0, "core")
        for half in (0, 1):
            for a in "xy":
                arrived(item(a, 2, 0), half)
                copy(item(a, 2, 0), item(a, 2, 1), half, "core")

    def finish():
        for half in (0, 1):
            arrived(1, half)
            for a in "xy":
                for d in (1, 3, 2):
                    arrived(item(a, d, 1), half)
        for c in started:
            c.wait_send()

    return start, relay, finish


def encode(out, value):
    g = value.shape[0]
    rows = out.shape[1]
    halves = [value[:, :, :LANES], value[:, :, LANES:]]
    most = jnp.concatenate(
        [jnp.max(jnp.abs(h), axis=1) for h in halves] + [jnp.zeros((rows - 2 * g, LANES), jnp.float32)], axis=0
    )
    level = jnp.ceil(jnp.log2(jnp.maximum(most, 1e-30)) * STEP)
    out[2 * g] = level.astype(jnp.int32).astype(jnp.int16)
    inverse = jnp.exp2(level * (-1.0 / STEP)) * TOP
    for k in range(2):
        scaled = jnp.round(halves[k] * inverse[k * g : (k + 1) * g][:, None, :])
        out[k * g : (k + 1) * g] = scaled.astype(jnp.int32).astype(jnp.int16)


def scales(code):
    return jnp.exp2(code.astype(jnp.int32).astype(jnp.float32) * (1.0 / STEP)) * (1.0 / TOP)


def decode(ref):
    g = ref.shape[0] // 2
    scale = scales(ref[2 * g])
    tiles = ref[: 2 * g].astype(jnp.int32).astype(jnp.float32) * scale[: 2 * g][:, None, :]
    return jnp.concatenate([tiles[:g], tiles[g:]], axis=2)


def summed(value, axis):
    return jnp.sum(value, axis=axis, keepdims=True)


def balance(lo, hi):
    up = lax.broadcasted_iota(jnp.int32, (NODES, NODES), 0)
    across = lax.broadcasted_iota(jnp.int32, (NODES, NODES), 1)
    chip = lax.broadcasted_iota(jnp.int32, (NODES, lo.shape[1]), 0)
    is_lo = (chip == lo).astype(jnp.float32)
    is_hi = (chip == hi).astype(jnp.float32)
    lanes = (((1,), (1,)), ((), ()))
    count = lax.dot_general(is_lo, is_hi, lanes, preferred_element_type=jnp.float32)
    count += lax.dot_general(is_hi, is_lo, lanes, preferred_element_type=jnp.float32)
    same = up == across
    loops = jnp.where(same, count * 0.5, 0.0)
    count = jnp.where(same, 0.0, count)
    loops_up, loops_across = summed(loops, 1), summed(loops, 0)

    def loads(give):
        return summed(give, 1) + loops_up, summed(count - give, 0) + loops_across

    give = count * 0.5
    for _ in range(BALANCE):
        load_up, load_across = loads(give)
        give = jnp.clip(give - (load_up - load_across) * (1.0 / NODES), 0.0, count)
    give = jnp.where(up < across, jnp.floor(give + 0.5), count - jnp.floor(count - give + 0.5))
    tag_up, tag_across = up.astype(jnp.float32), across.astype(jnp.float32)
    for _ in range(FIXES):
        load_up, load_across = loads(give)
        full_up, full_across = load_up * 64.0 + tag_up, load_across * 64.0 + tag_across
        full = jnp.max(jnp.max(full_across, axis=1, keepdims=True), axis=0, keepdims=True)
        target = jnp.where((full_up == full) & (give > 0.0), full_across, 1e9)
        mirror = jnp.where((full_across == full) & (count - give > 0.0), full_up, 1e9)
        least = jnp.min(jnp.min(target, axis=1, keepdims=True), axis=0, keepdims=True)
        move = (full - least >= 128.0).astype(jnp.float32)
        give = give - jnp.where(target == least, move, 0.0) + jnp.where(mirror == least, move, 0.0)
    load_up, load_across = loads(give)
    most = jnp.max(load_across, axis=1, keepdims=True)
    return give, is_lo, is_hi, most


def earlier(key):
    n = key.shape[1]
    up = lax.broadcasted_iota(jnp.int32, (n, n), 0)
    across = lax.broadcasted_iota(jnp.int32, (n, n), 1)
    column = summed(jnp.where(up == across, key, 0), 1)
    return summed(jnp.where((column == key) & (up < across), 1, 0), 0), column, up == across


def tables(pairs, turn):
    y, x, q = place()
    r, c = pairs[0:1, :], pairs[1:2, :]
    yr, xr, yc, xc = r >> 3, (r >> 1) & 3, c >> 3, (c >> 1) & 3
    one, two = yr * NX + xc, yc * NX + xr
    lo, hi = jnp.minimum(one, two), jnp.maximum(one, two)
    give, is_lo, is_hi, most = balance(lo, hi)
    share = lax.dot_general(give, is_lo, (((0,), (0,)), ((), ())), preferred_element_type=jnp.float32)
    share = summed(share * is_hi, 0)
    rank = earlier(lo * NODES + hi)[0]
    node = jnp.where(rank.astype(jnp.float32) < share, lo, hi)
    rank, node, same = earlier(node)

    def column(v):
        return summed(jnp.where(same, v, 0), 1)

    r, c, rank = column(r), column(c), column(rank)
    core, slot = rank & 1, (rank >> 1) - turn * SLOTS
    lane = lax.broadcasted_iota(jnp.int32, (r.shape[0], LANES), 1)

    def seen(block_y, block_x, other):
        along = 2 * ((block_x - x) & (NX - 1)) + other
        across = jnp.where(block_y == y, 0, 2 * NX - 2) + 2 * ((block_y - y) & (NY - 1)) + other
        return jnp.where(block_y == y, along, across)

    pick = (node == y * NX + x) & (core == q) & (slot == lane)
    rows = summed(jnp.where(pick, seen(r >> 3, (r >> 1) & 3, (r & 1) ^ q), 0), 0)
    cols = summed(jnp.where(pick, seen(c >> 3, (c >> 1) & 3, (c & 1) ^ q), 0), 0)
    want = (r == (y * NX + x) * 2 + q) & (slot >= 0) & (slot < SLOTS) & (c == lane)
    src = summed(jnp.where(want, seen(node >> 2, node & 3, core ^ q), 0), 0)
    at = summed(jnp.where(want, slot, 0), 0)
    live = summed(jnp.where(want, 1, 0), 0)
    rows, cols, src = [jnp.minimum(v, ITEMS - 1) for v in (rows, cols, src)]
    return (rows, cols, src, jnp.minimum(at, SLOTS - 1), live), most


def trees(nz):
    far = (nz // 2, nz // 2 - 1)
    if PATTERN == "ring":
        return [{k: k - 1 for k in range(1, n + 1)} for n in far]
    return [{k: max(k - 2 + k % 2, 0) for k in range(1, n + 1)} for n in far]


def kernel(
    nz, turn, pairs, factors, out, most_out, blocks, partial, z_out, z_in, parts, scale, table, table_s,
    local, gsend, grecv, zsend, zrecv, xsend, xrecv,
):
    z = lax.axis_index("narrow")
    rows = blocks.shape[2]
    chunk = rows // nz
    tree = trees(nz)
    starts = [sum(STREAMS[:s]) for s in range(len(STREAMS))]

    def away(d):
        return {"narrow": lax.rem(z + d + nz, nz)}

    own = pltpu.make_async_copy(factors, blocks.at[0], local)
    own.start()
    barrier = pltpu.get_barrier_semaphore()
    hops = sorted({sign * (k - p) for t in tree for k, p in t.items() for sign in (1, -1)})
    peers = list(neighbours().values()) + [away(d) for d in hops]
    for peer in peers:
        pl.semaphore_signal(barrier, inc=1, device_id=peer, device_id_type=MESH)
    own.wait()
    pl.semaphore_wait(barrier, len(peers))

    start, relay, finish = cross_gather(blocks, ((0,), (1,)), gsend, grecv)
    start()
    lists, most = tables(pairs[...], turn[0])
    for k, v in enumerate(lists):
        table[k : k + 1, :] = v
    most_out[...] = jnp.broadcast_to(most, most_out.shape)
    scalars = pltpu.make_async_copy(table, table_s, local)
    scalars.start()
    relay()
    scalars.wait()
    finish()

    def make(s, _):
        i, j = table_s[0, s], table_s[1, s]
        contract = (((1,), (1,)), ((), ()))
        partial[s] = lax.dot_general(
            blocks[i, 0], blocks[j, 0], contract, preferred_element_type=jnp.float32
        ) + lax.dot_general(blocks[i, 1], blocks[j, 1], contract, preferred_element_type=jnp.float32)
        return 0

    def span(stream):
        at = 2 * starts[stream] + stream
        return pl.ds(at, 2 * STREAMS[stream] + 1)

    def mine(dest, stream):
        at = pl.multiple_of(dest * chunk, chunk)
        return partial[pl.ds(starts[stream], STREAMS[stream]), pl.ds(at, chunk), :]

    def hop(side, k, stream):
        buf = side * (nz // 2) + k - 1
        return pltpu.make_async_remote_copy(
            src_ref=z_out.at[buf, span(stream)],
            dst_ref=z_in.at[buf, span(stream)],
            send_sem=zsend.at[buf, stream],
            recv_sem=zrecv.at[buf, stream],
            device_id=away((1, -1)[side] * (k - tree[side][k])),
            device_id_type=MESH,
        )

    sent = []

    def gathered(side, k, stream, value):
        for child, parent in sorted(tree[side].items(), reverse=True):
            if parent == k:
                hop(side, child, stream).wait_recv()
                value += decode(z_in.at[side * (nz // 2) + child - 1, span(stream)])
        return value

    def send(side, k, stream):
        dest = lax.rem(z + (1, -1)[side] * k + nz, nz)
        value = gathered(side, k, stream, mine(dest, stream))
        encode(z_out.at[side * (nz // 2) + k - 1, span(stream)], value)
        c = hop(side, k, stream)
        c.start()
        sent.append(c)

    for k in range(nz // 2, 0, -1):
        for stream in range(len(STREAMS)):
            if k == nz // 2:
                lax.fori_loop(starts[stream], starts[stream] + STREAMS[stream], make, 0)
            for side in (0, 1):
                if k in tree[side]:
                    send(side, k, stream)
    for stream in range(len(STREAMS)):
        value = mine(z, stream)
        for side in (1, 0):
            value = gathered(side, 0, stream, value)
        encode(parts.at[0, span(stream)], value)

    tiles = parts.shape[1]
    cut = tiles // 2
    start, relay, finish = cross_gather(parts, ((pl.ds(0, cut),), (pl.ds(cut, tiles - cut),)), xsend, xrecv)
    start()
    relay()
    finish()
    for k in range(ITEMS):
        for stream, g in enumerate(STREAMS):
            s = scales(parts[k, 2 * starts[stream] + stream + 2 * g])
            for j in range(g):
                scale[k * SLOTS + starts[stream] + j, 0:1, :] = s[j : j + 1]
                scale[k * SLOTS + starts[stream] + j, 1:2, :] = s[g + j : g + j + 1]
    nblk = out.shape[1] // rows
    for c in range(nblk):
        src, slot, live = table_s[2, c], table_s[3, c], table_s[4, c]
        first, step = slot, STREAMS[0]
        for stream in range(1, len(STREAMS)):
            later = slot >= starts[stream]
            first = jnp.where(later, slot + starts[stream] + stream, first)
            step = jnp.where(later, STREAMS[stream], step)
        s = scale[src * SLOTS + slot]
        for h in range(2):
            tile = parts[src, first + h * step].astype(jnp.int32).astype(jnp.float32) * s[h : h + 1]
            out[:, c * rows + h * LANES : c * rows + (h + 1) * LANES] = jnp.where(live > 0, tile, 0.0)
    for c in sent:
        c.wait_send()


def shards(factors, pairs):
    nz = lax.axis_size("narrow")
    two, rows, occ = factors.shape
    nblk = lax.axis_size("wide")
    chunk = rows // nz
    tiles = 2 * SLOTS + len(STREAMS)
    hops = (nz - 1, len(STREAMS))
    pairs = pairs.T

    def run(turn):
        return pl.pallas_call(
            functools.partial(kernel, nz),
            out_shape=(
                jax.ShapeDtypeStruct((chunk, nblk * rows), jnp.float32),
                jax.ShapeDtypeStruct((8, LANES), jnp.float32),
            ),
            in_specs=[
                pl.BlockSpec(memory_space=pltpu.SMEM),
                pl.BlockSpec(memory_space=pltpu.VMEM),
                pl.BlockSpec(memory_space=pl.ANY),
            ],
            out_specs=[pl.BlockSpec(memory_space=pltpu.VMEM)] * 2,
            scratch_shapes=[
                pltpu.VMEM((ITEMS, two, rows, occ), jnp.bfloat16),
                pltpu.VMEM((SLOTS, rows, rows), jnp.float32),
                pltpu.VMEM((nz - 1, tiles, chunk, LANES), jnp.int16),
                pltpu.VMEM((nz - 1, tiles, chunk, LANES), jnp.int16),
                pltpu.VMEM((ITEMS, tiles, chunk, LANES), jnp.int16),
                pltpu.VMEM((ITEMS * SLOTS, 8, LANES), jnp.float32),
                pltpu.VMEM((8, LANES), jnp.int32),
                pltpu.SMEM((8, LANES), jnp.int32),
                pltpu.SemaphoreType.DMA,
                pltpu.SemaphoreType.DMA((2 * ITEMS - 2,)),
                pltpu.SemaphoreType.DMA((ITEMS, 2)),
                pltpu.SemaphoreType.DMA(hops),
                pltpu.SemaphoreType.DMA(hops),
                pltpu.SemaphoreType.DMA((2 * ITEMS - 2,)),
                pltpu.SemaphoreType.DMA((ITEMS, 2)),
            ],
            compiler_params=pltpu.CompilerParams(
                collective_id=0, has_side_effects=True, vmem_limit_bytes=48 * 1024 * 1024
            ),
        )(turn, pairs, factors)

    out, most = run(jnp.zeros((1,), jnp.int32))
    most = most[0, 0]

    def more(state):
        return state[0].astype(jnp.float32) * (2 * SLOTS) < most

    def again(state):
        turn, out = state
        return turn + 1, out + run(turn[None])[0]

    return lax.while_loop(more, again, (jnp.int32(1), out))[1]


def solution(mesh):
    placed = (P("narrow", "wide", None), P())
    return jax.shard_map(
        shards, mesh=mesh, in_specs=placed, out_specs=P(("wide", "narrow"), None), check_vma=False
    )
```

time: 224 us -> 77.5 us (0.35)
  the two profiles are of different devices: /device:TPU:12 before, /device:TPU:1 now
where the time goes in v2:
time: 77.5 us; the launch traced here: 77.3 us
  Pallas kernels  74.7 us (96%)
  local copies, waits for them, and re-layouts  1.98 us (3%)
    pallas_call x1, Pallas kernels, run(): pl.pallas_call(functools.partial(kernel, nz), out_shape=(jax.ShapeDtypeSt...  74.7 us

profile of v2, /device:TPU:1, one launch (start us, length us, event | category | flops | bytes accessed | tf_op | source)
XLA Modules:
  0.0 77.3 jit_solution(17519345653285739620)
XLA Ops:
  0.0 0.0 copy-start
  0.0 74.7 %shard_map.28 = (f32[16,8192]{1,0:T(8,128)S(1)}, f32[8,128]{1,0:T(8,128)S(1)}) custom-call(s32[1]{0:T(128)} %constant.4.clone.1.turn, s32[2,256]{1,0:T(2,128)} %bitcast.5, bf16[2,256,512]{2,1,0:T(8,128)(2,1)} %factors.1), custom_call_target="tpu_custom_call" | custom-call | tf_op jit(solution)/shard_map/pallas_call | solution.py:364
  74.7 0.5 slice.3
  75.2 0.0 copy-start.1
  75.2 0.0 copy-done
  75.2 0.7 copy-done.1
  75.9 0.6 while.10
  76.5 0.8 %copy.10 = f32[16,8192]{1,0:T(8,128)} copy(f32[16,8192]{1,0:T(8,128)S(1)} %get-tuple-element.38) | data formatting | bytes 1048576
Async XLA Ops:
  0.0 75.2 %copy-start = (bf16[2,256,512]{2,1,0:T(8,128)(2,1)S(1)}, bf16[2,256,512]{2,1,0:T(8,128)(2,1)}, u32[]{:S(2)}) copy-start(bf16[2,256,512]{2,1,0:T(8,128)(2,1)} %factors.1) | copy-start | bytes 1572868
  75.2 0.7 copy-start.1

commit v3 on v2

v3 whole, which is shorter than its diff:
```python
import functools

import jax
import jax.numpy as jnp
from jax import lax
from jax.experimental import pallas as pl
from jax.experimental.pallas import tpu as pltpu
from jax.sharding import PartitionSpec as P

MESH = pl.DeviceIdType.MESH
NX = NY = 4
NODES = NX * NY
EARLY, LATE = (5,), (4,)
STREAMS = EARLY + LATE
HEAD, TAIL = sum(EARLY), sum(LATE)
SLOTS = HEAD + TAIL
LANES = 128
STEP = 16.0
TOP = 32000.0
ROUTES = ("skip", 0), ("skip", 1)
STEPS = (0, (6, 3)), (1, (6, 3)), (0, (4, 1)), (1, (4, 1)), (0, (2,)), (1, (2,))
FIRST = (8, 7, 5), (8, 7, 5)
BALANCE, FIXES = 4, 6


def place():
    w = lax.axis_index("wide")
    return w // (2 * NX), lax.rem(w // 2, NX), lax.rem(w, 2)


def wide(y, x, q):
    return {"wide": (y * NX + x) * 2 + q}


NEAR = 10


def item(axis, distance, other):
    if distance == 0:
        return other
    if distance == 2:
        return NEAR + "xy".index(axis) * 2 + other
    return 2 + "xy".index(axis) * 4 + (distance - 1) + other


ITEMS = 2 * (NX + NY - 1)


def neighbours():
    y, x, q = place()
    return {
        ("x", 1): wide(y, lax.rem(x + 1, NX), q),
        ("x", -1): wide(y, lax.rem(x + NX - 1, NX), q),
        ("y", 1): wide(lax.rem(y + 1, NY), x, q),
        ("y", -1): wide(lax.rem(y + NY - 1, NY), x, q),
        ("x", 2): wide(y, lax.rem(x + 2, NX), q),
        ("y", 2): wide(lax.rem(y + 2, NY), x, q),
        "core": wide(y, x, 1 - q),
    }


def courier(view, pieces, send, recv):
    near = neighbours()
    started = []

    def both(src, dst, piece, to, sem):
        cut, at = pieces[piece]
        return pltpu.make_async_remote_copy(
            src_ref=view(src, cut),
            dst_ref=view(dst, cut),
            send_sem=send.at[sem],
            recv_sem=recv.at[dst, at],
            device_id=near[to],
            device_id_type=MESH,
        )

    def copy(src, dst, piece, to):
        c = both(src, dst, piece, to, len(started))
        c.start()
        started.append(c)

    def arrived(dst, piece):
        both(dst, dst, piece, "core", 0).wait_recv()

    def drain():
        for c in started:
            c.wait_send()

    return copy, arrived, drain


def gather_blocks(close, distant, send, recv):
    def view(k, cut):
        return close.at[(k,) + cut] if k < NEAR else distant.at[(k - NEAR,) + cut]

    copy, arrived, drain = courier(view, (((0,), 0), ((1,), 1)), send, recv)

    def start():
        for first in (0, 1):
            for a in "xy":
                copy(0, item(a, 3, 0), first, (a, 1))
                copy(0, item(a, 1, 0), 1 - first, (a, -1))
        for half in (0, 1):
            copy(0, 1, half, "core")

    def relay():
        for a in "xy":
            arrived(item(a, 3, 0), 0)
            copy(item(a, 3, 0), item(a, 2, 0), 0, (a, 1))
            arrived(item(a, 1, 0), 1)
            copy(item(a, 1, 0), item(a, 2, 0), 1, (a, -1))
        for a in "xy":
            copy(item(a, 3, 0), item(a, 3, 1), 0, "core")
            copy(item(a, 1, 0), item(a, 1, 1), 1, "core")

    def near():
        for a in "xy":
            arrived(item(a, 3, 0), 1)
            copy(item(a, 3, 0), item(a, 3, 1), 1, "core")
            arrived(item(a, 1, 0), 0)
            copy(item(a, 1, 0), item(a, 1, 1), 0, "core")
        for half in (0, 1):
            arrived(1, half)
            for a in "xy":
                arrived(item(a, 1, 1), half)
                arrived(item(a, 3, 1), half)

    def far():
        for half in (0, 1):
            for a in "xy":
                arrived(item(a, 2, 0), half)
                copy(item(a, 2, 0), item(a, 2, 1), half, "core")

    def finish():
        for half in (0, 1):
            for a in "xy":
                arrived(item(a, 2, 1), half)
        drain()

    return start, relay, near, far, finish


def exchange(buf, first, size, send, recv):
    cut = size // 2
    pieces = ((pl.ds(first, size),), 0), ((pl.ds(first, cut),), 0), ((pl.ds(first + cut, size - cut),), 1)
    copy, arrived, drain = courier(lambda k, cut: buf.at[(k,) + cut], pieces, send, recv)

    def start():
        for a in "xy":
            copy(0, item(a, 2, 0), 0, (a, 2))
        for a in "xy":
            copy(0, item(a, 3, 0), 0, (a, 1))
            copy(0, item(a, 1, 0), 0, (a, -1))
        copy(0, 1, 0, "core")

    def relay():
        for a in "xy":
            arrived(item(a, 3, 0), 0)
            copy(item(a, 3, 0), item(a, 3, 1), 0, "core")
            arrived(item(a, 1, 0), 0)
            copy(item(a, 1, 0), item(a, 1, 1), 0, "core")

    def far():
        for a in "xy":
            arrived(item(a, 2, 0), 0)
            copy(item(a, 2, 0), item(a, 2, 1), 0, "core")

    def finish():
        arrived(1, 0)
        for a in "xy":
            for d in (1, 3, 2):
                arrived(item(a, d, 1), 0)
        drain()

    return start, relay, far, finish


def encode(out, value):
    g = value.shape[0]
    rows = out.shape[1]
    halves = [value[:, :, :LANES], value[:, :, LANES:]]
    most = jnp.concatenate(
        [jnp.max(jnp.abs(h), axis=1) for h in halves] + [jnp.zeros((rows - 2 * g, LANES), jnp.float32)], axis=0
    )
    level = jnp.ceil(jnp.log2(jnp.maximum(most, 1e-30)) * STEP)
    out[2 * g] = level.astype(jnp.int32).astype(jnp.int16)
    inverse = jnp.exp2(level * (-1.0 / STEP)) * TOP
    for k in range(2):
        scaled = jnp.round(halves[k] * inverse[k * g : (k + 1) * g][:, None, :])
        out[k * g : (k + 1) * g] = scaled.astype(jnp.int32).astype(jnp.int16)


def scales(code):
    return jnp.exp2(code.astype(jnp.int32).astype(jnp.float32) * (1.0 / STEP)) * (1.0 / TOP)


def decode(ref):
    g = ref.shape[0] // 2
    scale = scales(ref[2 * g])
    tiles = ref[: 2 * g].astype(jnp.int32).astype(jnp.float32) * scale[: 2 * g][:, None, :]
    return jnp.concatenate([tiles[:g], tiles[g:]], axis=2)


def summed(value, axis):
    return jnp.sum(value, axis=axis, keepdims=True)


def balance(lo, hi, chosen):
    up = lax.broadcasted_iota(jnp.int32, (NODES, NODES), 0)
    across = lax.broadcasted_iota(jnp.int32, (NODES, NODES), 1)
    chip = lax.broadcasted_iota(jnp.int32, (NODES, lo.shape[1]), 0)
    is_lo = ((chip == lo) & chosen).astype(jnp.float32)
    is_hi = ((chip == hi) & chosen).astype(jnp.float32)
    lanes = (((1,), (1,)), ((), ()))
    count = lax.dot_general(is_lo, is_hi, lanes, preferred_element_type=jnp.float32)
    count += lax.dot_general(is_hi, is_lo, lanes, preferred_element_type=jnp.float32)
    same = up == across
    loops = jnp.where(same, count * 0.5, 0.0)
    count = jnp.where(same, 0.0, count)
    loops_up, loops_across = summed(loops, 1), summed(loops, 0)

    def loads(give):
        return summed(give, 1) + loops_up, summed(count - give, 0) + loops_across

    give = count * 0.5
    for _ in range(BALANCE):
        load_up, load_across = loads(give)
        give = jnp.clip(give - (load_up - load_across) * (1.0 / NODES), 0.0, count)
    give = jnp.where(up < across, jnp.floor(give + 0.5), count - jnp.floor(count - give + 0.5))
    tag_up, tag_across = up.astype(jnp.float32), across.astype(jnp.float32)
    for _ in range(FIXES):
        load_up, load_across = loads(give)
        full_up, full_across = load_up * 64.0 + tag_up, load_across * 64.0 + tag_across
        full = jnp.max(jnp.max(full_across, axis=1, keepdims=True), axis=0, keepdims=True)
        target = jnp.where((full_up == full) & (give > 0.0), full_across, 1e9)
        mirror = jnp.where((full_across == full) & (count - give > 0.0), full_up, 1e9)
        least = jnp.min(jnp.min(target, axis=1, keepdims=True), axis=0, keepdims=True)
        move = (full - least >= 128.0).astype(jnp.float32)
        give = give - jnp.where(target == least, move, 0.0) + jnp.where(mirror == least, move, 0.0)
    share = lax.dot_general(give, is_lo, (((0,), (0,)), ((), ())), preferred_element_type=jnp.float32)
    return summed(share * is_hi, 0)


def tables(pairs, turn):
    y, x, q = place()
    n = pairs.shape[1]
    up = lax.broadcasted_iota(jnp.int32, (n, n), 0)
    across = lax.broadcasted_iota(jnp.int32, (n, n), 1)
    same, before = up == across, up < across

    def column(v):
        return summed(jnp.where(same, v, 0), 1)

    def ranks(key):
        return summed(jnp.where((column(key) == key) & before, 1, 0), 0)

    r, c = pairs[0:1, :], pairs[1:2, :]
    yr, xr, yc, xc = r >> 3, (r >> 1) & 3, c >> 3, (c >> 1) & 3
    far_x, far_y = ((xr - xc) & 3) == 2, ((yr - yc) & 3) == 2
    middle_x, middle_y = far_x & (yr == yc), far_y & (xr == xc)
    late = (far_x | far_y) & jnp.logical_not(middle_x | middle_y)
    kind = late.astype(jnp.int32)
    one, two = yr * NX + xc, yc * NX + xr
    one = jnp.where(middle_x, yr * NX + ((xr + 1) & 3), jnp.where(middle_y, ((yr + 1) & 3) * NX + xr, one))
    two = jnp.where(middle_x, yr * NX + ((xr + 3) & 3), jnp.where(middle_y, ((yr + 3) & 3) * NX + xr, two))
    lo, hi = jnp.minimum(one, two), jnp.maximum(one, two)
    share = jnp.where(late, balance(lo, hi, late), balance(lo, hi, jnp.logical_not(late)))
    rank = ranks((lo * NODES + hi) * 2 + kind)
    node = jnp.where(rank.astype(jnp.float32) < share, lo, hi)
    rank = ranks(node * 2 + kind)
    node_up = column(node)
    ahead = summed(jnp.where((node_up == node) & (column(kind) == 0), 1, 0), 0)
    rank = jnp.where(late, jnp.maximum(ahead, 2 * HEAD) + rank, rank)
    most = jnp.broadcast_to(jnp.max(rank, axis=1, keepdims=True) + 1, (1, LANES))

    r, c, node, rank = column(r), column(c), node_up, column(rank)
    core, slot = rank & 1, (rank >> 1) - turn * TAIL
    inside = (slot >= jnp.where(turn > 0, HEAD, 0)) & (slot < SLOTS)
    lane = lax.broadcasted_iota(jnp.int32, (r.shape[0], LANES), 1)

    def seen(block_y, block_x, other):
        aside = block_y != y
        d = jnp.where(aside, block_y - y, block_x - x) & 3
        line = aside.astype(jnp.int32)
        return other + jnp.where(d == 0, 0, jnp.where(d == 2, NEAR + 2 * line, 1 + 4 * line + d))

    pick = (node == y * NX + x) & (core == q) & inside & (slot == lane)
    rows = summed(jnp.where(pick, seen(r >> 3, (r >> 1) & 3, (r & 1) ^ q), 0), 0)
    cols = summed(jnp.where(pick, seen(c >> 3, (c >> 1) & 3, (c & 1) ^ q), 0), 0)
    want = (r == (y * NX + x) * 2 + q) & inside & (c == lane)
    src = summed(jnp.where(want, seen(node >> 2, node & 3, core ^ q), 0), 0)
    at = summed(jnp.where(want, slot, 0), 0)
    live = summed(jnp.where(want, 1, 0), 0)
    rows, cols, src = [jnp.minimum(v, ITEMS - 1) for v in (rows, cols, src)]
    return rows, cols, src, jnp.minimum(at, SLOTS - 1), live, most


PARENTS = {
    "ring": {k: k - 1 for k in range(1, 9)},
    "skip": {8: 6, 7: 6, 6: 4, 5: 4, 4: 2, 3: 2, 2: 0, 1: 0},
    "mix": {8: 6, 7: 6, 6: 4, 5: 4, 4: 2, 3: 2, 2: 1, 1: 0},
}


def trees(group):
    pattern, longer = ROUTES[group]
    return [{k: p for k, p in PARENTS[pattern].items() if k < 8 or side == longer} for side in (0, 1)]


def kernel(
    nz, turn, pairs, factors, out, most_out, close, distant, partial, z_out, z_in, parts, scale, table, table_s,
    local, gsend, grecv, zsend, zrecv, xsend, xrecv,
):
    z = lax.axis_index("narrow")
    rows = close.shape[2]
    chunk = rows // nz
    forest = [trees(0)] * len(EARLY) + [trees(1)] * len(LATE)
    starts = [sum(STREAMS[:s]) for s in range(len(STREAMS))]

    def away(d):
        return {"narrow": lax.rem(z + d + nz, nz)}

    own = pltpu.make_async_copy(factors, close.at[0], local)
    own.start()
    barrier = pltpu.get_barrier_semaphore()
    hops = sorted({sign * (k - p) for trees in forest for t in trees for k, p in t.items() for sign in (1, -1)})
    peers = list(neighbours().values()) + [away(d) for d in hops]
    for peer in peers:
        pl.semaphore_signal(barrier, inc=1, device_id=peer, device_id_type=MESH)
    own.wait()
    pl.semaphore_wait(barrier, len(peers))

    start, relay, near, far, finish = gather_blocks(close, distant, gsend, grecv)
    start()
    for k, v in enumerate(tables(pairs[...], turn[0])):
        table[k : k + 1, :] = v
    scalars = pltpu.make_async_copy(table, table_s, local)
    scalars.start()
    relay()
    scalars.wait()
    most_out[0] = table_s[5, 0]

    def tile(s, load):
        i, j = table_s[0, s], table_s[1, s]
        contract = (((1,), (1,)), ((), ()))
        partial[s] = sum(
            lax.dot_general(load(i, p), load(j, p), contract, preferred_element_type=jnp.float32) for p in (0, 1)
        )

    def load_close(i, p):
        return close[jnp.minimum(i, NEAR - 1), p]

    def load_any(i, p):
        return jnp.where(i < NEAR, load_close(i, p), distant[jnp.maximum(i - NEAR, 0), p])

    def span(stream):
        at = 2 * starts[stream] + stream
        return pl.ds(at, 2 * STREAMS[stream] + 1)

    def mine(dest, stream):
        at = pl.multiple_of(dest * chunk, chunk)
        return partial[pl.ds(starts[stream], STREAMS[stream]), pl.ds(at, chunk), :]

    def hop(side, k, stream):
        buf = side * (nz // 2) + k - 1
        return pltpu.make_async_remote_copy(
            src_ref=z_out.at[buf, span(stream)],
            dst_ref=z_in.at[buf, span(stream)],
            send_sem=zsend.at[buf, stream],
            recv_sem=zrecv.at[buf, stream],
            device_id=away((1, -1)[side] * (k - forest[stream][side][k])),
            device_id_type=MESH,
        )

    sent = []

    def gathered(side, k, stream, value):
        for child, parent in sorted(forest[stream][side].items(), reverse=True):
            if parent == k:
                hop(side, child, stream).wait_recv()
                value += decode(z_in.at[side * (nz // 2) + child - 1, span(stream)])
        return value

    def send(side, k, stream):
        dest = lax.rem(z + (1, -1)[side] * k + nz, nz)
        value = gathered(side, k, stream, mine(dest, stream))
        encode(z_out.at[side * (nz // 2) + k - 1, span(stream)], value)
        c = hop(side, k, stream)
        c.start()
        sent.append(c)

    def leg(ks, streams):
        for stream in streams:
            for k in ks:
                for side in (0, 1):
                    if k in forest[stream][side]:
                        send(side, k, stream)

    def make(streams, load):
        def one(s, _):
            tile(s, load)
            return 0

        for stream in streams:
            lax.fori_loop(starts[stream], starts[stream] + STREAMS[stream], one, 0)

    groups = (range(len(EARLY)), range(len(EARLY), len(STREAMS)))
    near()
    make(groups[0], load_close)
    leg(FIRST[0], groups[0])
    far()
    finish()
    make(groups[1], load_any)
    leg(FIRST[1], groups[1])
    for group, ks in STEPS:
        leg(ks, groups[group])
    swaps = []
    for stream, g in enumerate(STREAMS):
        value = mine(z, stream)
        for side in (1, 0):
            value = gathered(side, 0, stream, value)
        encode(parts.at[0, span(stream)], value)
        swaps.append(exchange(parts, 2 * starts[stream] + stream, 2 * g + 1, xsend.at[stream], xrecv.at[stream]))
        swaps[-1][0]()
    for swap in swaps:
        swap[1]()
    for swap in swaps:
        swap[2]()
    for swap in swaps:
        swap[3]()
    for k in range(ITEMS):
        for stream, g in enumerate(STREAMS):
            s = scales(parts[k, 2 * starts[stream] + stream + 2 * g])
            for j in range(g):
                scale[k * SLOTS + starts[stream] + j, 0:1, :] = s[j : j + 1]
                scale[k * SLOTS + starts[stream] + j, 1:2, :] = s[g + j : g + j + 1]
    nblk = out.shape[1] // rows
    for c in range(nblk):
        src, slot, live = table_s[2, c], table_s[3, c], table_s[4, c]
        first, step = slot, STREAMS[0]
        for stream in range(1, len(STREAMS)):
            later = slot >= starts[stream]
            first = jnp.where(later, slot + starts[stream] + stream, first)
            step = jnp.where(later, STREAMS[stream], step)
        s = scale[src * SLOTS + slot]
        for h in range(2):
            found = parts[src, first + h * step].astype(jnp.int32).astype(jnp.float32) * s[h : h + 1]
            out[:, c * rows + h * LANES : c * rows + (h + 1) * LANES] = jnp.where(live > 0, found, 0.0)
    for c in sent:
        c.wait_send()


def shards(factors, pairs):
    nz = lax.axis_size("narrow")
    two, rows, occ = factors.shape
    nblk = lax.axis_size("wide")
    chunk = rows // nz
    tiles = 2 * SLOTS + len(STREAMS)
    hops = (nz, len(STREAMS))
    pairs = pairs.T

    def run(turn):
        return pl.pallas_call(
            functools.partial(kernel, nz),
            out_shape=(
                jax.ShapeDtypeStruct((chunk, nblk * rows), jnp.float32),
                jax.ShapeDtypeStruct((1,), jnp.int32),
            ),
            in_specs=[
                pl.BlockSpec(memory_space=pltpu.SMEM),
                pl.BlockSpec(memory_space=pltpu.VMEM),
                pl.BlockSpec(memory_space=pl.ANY),
            ],
            out_specs=[pl.BlockSpec(memory_space=pltpu.VMEM), pl.BlockSpec(memory_space=pltpu.SMEM)],
            scratch_shapes=[
                pltpu.VMEM((NEAR, two, rows, occ), jnp.bfloat16),
                pltpu.VMEM((ITEMS - NEAR, two, rows, occ), jnp.bfloat16),
                pltpu.VMEM((SLOTS, rows, rows), jnp.float32),
                pltpu.VMEM((nz, tiles, chunk, LANES), jnp.int16),
                pltpu.VMEM((nz, tiles, chunk, LANES), jnp.int16),
                pltpu.VMEM((ITEMS, tiles, chunk, LANES), jnp.int16),
                pltpu.VMEM((ITEMS * SLOTS, 8, LANES), jnp.float32),
                pltpu.VMEM((8, LANES), jnp.int32),
                pltpu.SMEM((8, LANES), jnp.int32),
                pltpu.SemaphoreType.DMA,
                pltpu.SemaphoreType.DMA((2 * ITEMS - 2,)),
                pltpu.SemaphoreType.DMA((ITEMS, 2)),
                pltpu.SemaphoreType.DMA(hops),
                pltpu.SemaphoreType.DMA(hops),
                pltpu.SemaphoreType.DMA((len(STREAMS), 15)),
                pltpu.SemaphoreType.DMA((len(STREAMS), ITEMS, 2)),
            ],
            compiler_params=pltpu.CompilerParams(
                collective_id=0, has_side_effects=True, vmem_limit_bytes=48 * 1024 * 1024
            ),
        )(turn, pairs, factors)

    out, most = run(jnp.zeros((1,), jnp.int32))

    def more(state):
        return most[0] > 2 * (HEAD + state[0] * TAIL)

    def again(state):
        turn, out = state
        return turn + 1, out + run(turn[None])[0]

    return lax.while_loop(more, again, (jnp.int32(1), out))[1]


def solution(mesh):
    placed = (P("narrow", "wide", None), P())
    return jax.shard_map(
        shards, mesh=mesh, in_specs=placed, out_specs=P(("wide", "narrow"), None), check_vma=False
    )
```

time: 77.5 us -> 67.5 us (0.87)
  Pallas kernels: 74.7 us -> 65.1 us
    pallas_call x1, Pallas kernels: 74.7 us -> 65.1 us  [run(): pl.pallas_call(functools.partial(kernel, nz), out_shape=(jax.ShapeDtypeSt...]
where the time goes in v3:
time: 67.5 us; the launch traced here: 67.3 us
  Pallas kernels  65.1 us (96%)
  local copies, waits for them, and re-layouts  1.47 us (2%)
    pallas_call x1, Pallas kernels, run(): pl.pallas_call(functools.partial(kernel, nz), out_shape=(jax.ShapeDtypeSt...  65.1 us
    unnamed x5, local copies, waits for them, and re-layouts  1.47 us

profile of v3, /device:TPU:1, one launch (start us, length us, event | category | flops | bytes accessed | tf_op | source)
XLA Modules:
  0.0 67.3 jit_solution(8750979079613460512)
XLA Ops:
  0.0 0.0 copy-start
  0.0 65.1 %shard_map.28 = (f32[16,8192]{1,0:T(8,128)S(1)}, s32[1]{0:T(128)}) custom-call(s32[1]{0:T(128)} %constant.6.clone.1.turn, s32[2,256]{1,0:T(2,128)} %bitcast.6, bf16[2,256,512]{2,1,0:T(8,128)(2,1)} %factors.1), custom_call_target="tpu_custom_call" | custom-call | tf_op jit(solution)/shard_map/pallas_call | solution.py:463
  65.2 0.0 copy-start.1
  65.2 0.0 copy-done
  65.2 0.7 copy-done.1
  65.8 0.6 while.10
  66.5 0.8 %copy.10 = f32[16,8192]{1,0:T(8,128)} copy(f32[16,8192]{1,0:T(8,128)S(1)} %get-tuple-element.38) | data formatting | bytes 1048576
Async XLA Ops:
  0.0 65.2 %copy-start = (bf16[2,256,512]{2,1,0:T(8,128)(2,1)S(1)}, bf16[2,256,512]{2,1,0:T(8,128)(2,1)}, u32[]{:S(2)}) copy-start(bf16[2,256,512]{2,1,0:T(8,128)(2,1)} %factors.1) | copy-start | bytes 1572868
  65.2 0.7 %copy-start.1 = (s32[256,2]{0,1:T(2,128)S(1)}, s32[256,2]{0,1:T(2,128)}, u32[]{:S(2)}) copy-start(s32[256,2]{0,1:T(2,128)} %param.5) | copy-start | bytes 6148

commit v4 on v3

--- a/solution.py
+++ b/solution.py
@@ -309,7 +309,7 @@
 
 def kernel(
     nz, turn, pairs, factors, out, most_out, close, distant, partial, z_out, z_in, parts, scale, table, table_s,
-    local, gsend, grecv, zsend, zrecv, xsend, xrecv,
+    listed, listed_sem, local, gsend, grecv, zsend, zrecv, xsend, xrecv,
 ):
     z = lax.axis_index("narrow")
     rows = close.shape[2]
@@ -322,17 +322,20 @@
 
     own = pltpu.make_async_copy(factors, close.at[0], local)
     own.start()
+    listing = pltpu.make_async_copy(pairs, listed, listed_sem)
+    listing.start()
     barrier = pltpu.get_barrier_semaphore()
     hops = sorted({sign * (k - p) for trees in forest for t in trees for k, p in t.items() for sign in (1, -1)})
     peers = list(neighbours().values()) + [away(d) for d in hops]
     for peer in peers:
         pl.semaphore_signal(barrier, inc=1, device_id=peer, device_id_type=MESH)
     own.wait()
+    listing.wait()
     pl.semaphore_wait(barrier, len(peers))
 
     start, relay, near, far, finish = gather_blocks(close, distant, gsend, grecv)
     start()
-    for k, v in enumerate(tables(pairs[...], turn[0])):
+    for k, v in enumerate(tables(listed[...], turn[0])):
         table[k : k + 1, :] = v
     scalars = pltpu.make_async_copy(table, table_s, local)
     scalars.start()
@@ -409,10 +412,12 @@
     make(groups[0], load_close)
     leg(FIRST[0], groups[0])
     far()
+    leg((6,), groups[0])
     finish()
     make(groups[1], load_any)
     leg(FIRST[1], groups[1])
-    for group, ks in STEPS:
+    leg((3,), groups[0])
+    for group, ks in STEPS[1:]:
         leg(ks, groups[group])
     swaps = []
     for stream, g in enumerate(STREAMS):
@@ -468,7 +473,7 @@
             ),
             in_specs=[
                 pl.BlockSpec(memory_space=pltpu.SMEM),
-                pl.BlockSpec(memory_space=pltpu.VMEM),
+                pl.BlockSpec(memory_space=pl.ANY),
                 pl.BlockSpec(memory_space=pl.ANY),
             ],
             out_specs=[pl.BlockSpec(memory_space=pltpu.VMEM), pl.BlockSpec(memory_space=pltpu.SMEM)],
@@ -482,6 +487,8 @@
                 pltpu.VMEM((ITEMS * SLOTS, 8, LANES), jnp.float32),
                 pltpu.VMEM((8, LANES), jnp.int32),
                 pltpu.SMEM((8, LANES), jnp.int32),
+                pltpu.VMEM(pairs.shape, jnp.int32),
+                pltpu.SemaphoreType.DMA,
                 pltpu.SemaphoreType.DMA,
                 pltpu.SemaphoreType.DMA((2 * ITEMS - 2,)),
                 pltpu.SemaphoreType.DMA((ITEMS, 2)),
@@ -504,7 +511,10 @@
         turn, out = state
         return turn + 1, out + run(turn[None])[0]
 
-    return lax.while_loop(more, again, (jnp.int32(1), out))[1]
+    def rest(out):
+        return lax.while_loop(more, again, (jnp.int32(1), out))[1]
+
+    return lax.cond(most[0] > 2 * SLOTS, rest, lambda out: out, out)
 
 
 def solution(mesh):

time: 67.5 us -> 66 us (0.978)
  Pallas kernels: 65.1 us -> 63.7 us
  between operations: 0.03 us -> 0.72 us
    pallas_call x1, Pallas kernels: 65.1 us -> 63.7 us  [run(): pl.pallas_call(functools.partial(kernel, nz), out_shape=(jax.ShapeDtypeSt...]
where the time goes in v4:
time: 66 us; the launch traced here: 65.8 us
  Pallas kernels  63.7 us (97%)
  local copies, waits for them, and re-layouts  1.46 us (2%)
  between operations  0.72 us (1%)
    pallas_call x1, Pallas kernels, run(): pl.pallas_call(functools.partial(kernel, nz), out_shape=(jax.ShapeDtypeSt...  63.7 us
    unnamed x5, local copies, waits for them, and re-layouts  1.46 us

profile of v4, /device:TPU:1, one launch (start us, length us, event | category | flops | bytes accessed | tf_op | source)
XLA Modules:
  0.0 65.8 jit_solution(13380584426513356756)
XLA Ops:
  0.0 0.0 copy-start
  0.0 63.7 %shard_map.30 = (f32[16,8192]{1,0:T(8,128)S(1)}, s32[1]{0:T(128)}) custom-call(s32[1]{0:T(128)} %constant.7.clone.1.turn, s32[2,256]{1,0:T(2,128)} %bitcast.7, bf16[2,256,512]{2,1,0:T(8,128)(2,1)} %factors.1), custom_call_target="tpu_custom_call" | custom-call | tf_op jit(solution)/shard_map/pallas_call | solution.py:468
  64.4 0.0 copy-start.1
  64.4 0.0 copy-done
  64.4 0.7 %copy-done.1 = s32[256,2]{0,1:T(2,128)S(1)} copy-done((s32[256,2]{0,1:T(2,128)S(1)}, s32[256,2]{0,1:T(2,128)}, u32[]{:S(2)}) %copy-start.1) | copy-done | bytes 2072
  65.1 0.8 %copy.14 = f32[16,8192]{1,0:T(8,128)} copy(f32[16,8192]{1,0:T(8,128)S(1)} %get-tuple-element.54) | data formatting | bytes 1048576
  (1 shorter events, 0.0 us)
Async XLA Ops:
  0.0 64.4 %copy-start = (bf16[2,256,512]{2,1,0:T(8,128)(2,1)S(1)}, bf16[2,256,512]{2,1,0:T(8,128)(2,1)}, u32[]{:S(2)}) copy-start(bf16[2,256,512]{2,1,0:T(8,128)(2,1)} %factors.1) | copy-start | bytes 1572868
  64.4 0.7 %copy-start.1 = (s32[256,2]{0,1:T(2,128)S(1)}, s32[256,2]{0,1:T(2,128)}, u32[]{:S(2)}) copy-start(s32[256,2]{0,1:T(2,128)} %param.7) | copy-start | bytes 6148

commit v5 on v4

--- a/solution.py
+++ b/solution.py
@@ -63,10 +63,10 @@
     near = neighbours()
     started = []
 
-    def both(src, dst, piece, to, sem):
+    def both(src, dst, piece, to, sem, origin=None):
         cut, at = pieces[piece]
         return pltpu.make_async_remote_copy(
-            src_ref=view(src, cut),
+            src_ref=view(src, cut) if origin is None else origin.at[cut],
             dst_ref=view(dst, cut),
             send_sem=send.at[sem],
             recv_sem=recv.at[dst, at],
@@ -74,8 +74,8 @@
             device_id_type=MESH,
         )
 
-    def copy(src, dst, piece, to):
-        c = both(src, dst, piece, to, len(started))
+    def copy(src, dst, piece, to, origin=None):
+        c = both(src, dst, piece, to, len(started), origin)
         c.start()
         started.append(c)
 
@@ -89,7 +89,7 @@
     return copy, arrived, drain
 
 
-def gather_blocks(close, distant, send, recv):
+def gather_blocks(own, close, distant, send, recv):
     def view(k, cut):
         return close.at[(k,) + cut] if k < NEAR else distant.at[(k - NEAR,) + cut]
 
@@ -98,10 +98,10 @@
     def start():
         for first in (0, 1):
             for a in "xy":
-                copy(0, item(a, 3, 0), first, (a, 1))
-                copy(0, item(a, 1, 0), 1 - first, (a, -1))
+                copy(0, item(a, 3, 0), first, (a, 1), own)
+                copy(0, item(a, 1, 0), 1 - first, (a, -1), own)
         for half in (0, 1):
-            copy(0, 1, half, "core")
+            copy(0, 1, half, "core", own)
 
     def relay():
         for a in "xy":
@@ -308,7 +308,7 @@
 
 
 def kernel(
-    nz, turn, pairs, factors, out, most_out, close, distant, partial, z_out, z_in, parts, scale, table, table_s,
+    nz, turn, pairs, factors, out, again_out, echo, close, distant, partial, z_out, z_in, parts, scale, table, table_s,
     listed, listed_sem, local, gsend, grecv, zsend, zrecv, xsend, xrecv,
 ):
     z = lax.axis_index("narrow")
@@ -329,19 +329,20 @@
     peers = list(neighbours().values()) + [away(d) for d in hops]
     for peer in peers:
         pl.semaphore_signal(barrier, inc=1, device_id=peer, device_id_type=MESH)
+    pl.semaphore_wait(barrier, len(peers))
+
+    start, relay, near, far, finish = gather_blocks(factors, close, distant, gsend, grecv)
+    start()
+    listing.wait()
     own.wait()
-    listing.wait()
-    pl.semaphore_wait(barrier, len(peers))
-
-    start, relay, near, far, finish = gather_blocks(close, distant, gsend, grecv)
-    start()
     for k, v in enumerate(tables(listed[...], turn[0])):
         table[k : k + 1, :] = v
     scalars = pltpu.make_async_copy(table, table_s, local)
     scalars.start()
     relay()
     scalars.wait()
-    most_out[0] = table_s[5, 0]
+    again_out[0] = jnp.where(table_s[5, 0] > 2 * (HEAD + (turn[0] + 1) * TAIL), 1, 0)
+    echo[...] = listed[...]
 
     def tile(s, load):
         i, j = table_s[0, s], table_s[1, s]
@@ -464,19 +465,24 @@
     hops = (nz, len(STREAMS))
     pairs = pairs.T
 
-    def run(turn):
+    def run(pairs, turn):
         return pl.pallas_call(
             functools.partial(kernel, nz),
             out_shape=(
                 jax.ShapeDtypeStruct((chunk, nblk * rows), jnp.float32),
                 jax.ShapeDtypeStruct((1,), jnp.int32),
+                jax.ShapeDtypeStruct(pairs.shape, jnp.int32),
             ),
             in_specs=[
                 pl.BlockSpec(memory_space=pltpu.SMEM),
                 pl.BlockSpec(memory_space=pl.ANY),
                 pl.BlockSpec(memory_space=pl.ANY),
             ],
-            out_specs=[pl.BlockSpec(memory_space=pltpu.VMEM), pl.BlockSpec(memory_space=pltpu.SMEM)],
+            out_specs=[
+                pl.BlockSpec(memory_space=pltpu.VMEM),
+                pl.BlockSpec(memory_space=pltpu.SMEM),
+                pl.BlockSpec(memory_space=pltpu.VMEM),
+            ],
             scratch_shapes=[
                 pltpu.VMEM((NEAR, two, rows, occ), jnp.bfloat16),
                 pltpu.VMEM((ITEMS - NEAR, two, rows, occ), jnp.bfloat16),
@@ -498,23 +504,22 @@
                 pltpu.SemaphoreType.DMA((len(STREAMS), ITEMS, 2)),
             ],
             compiler_params=pltpu.CompilerParams(
-                collective_id=0, has_side_effects=True, vmem_limit_bytes=48 * 1024 * 1024
+                collective_id=0, has_side_effects=True, vmem_limit_bytes=62 * 1024 * 1024
             ),
         )(turn, pairs, factors)
 
-    out, most = run(jnp.zeros((1,), jnp.int32))
-
-    def more(state):
-        return most[0] > 2 * (HEAD + state[0] * TAIL)
-
-    def again(state):
-        turn, out = state
-        return turn + 1, out + run(turn[None])[0]
-
-    def rest(out):
-        return lax.while_loop(more, again, (jnp.int32(1), out))[1]
-
-    return lax.cond(most[0] > 2 * SLOTS, rest, lambda out: out, out)
+    out, more, pairs = run(pairs, jnp.zeros((1,), jnp.int32))
+
+    def rest(pairs, out):
+        def again(state):
+            turn, out, _, pairs = state
+            further, more, pairs = run(pairs, turn[None])
+            return turn + 1, out + further, more, pairs
+
+        state = (jnp.int32(1), out, jnp.ones((1,), jnp.int32), pairs)
+        return lax.while_loop(lambda state: state[2][0] > 0, again, state)[1]
+
+    return lax.switch(more[0], [lambda pairs, out: out, rest], pairs, out)
 
 
 def solution(mesh):

time: 66 us -> 65.5 us (level)
    unnamed x5 -> x3, local copies, waits for them, and re-layouts: 1.46 us -> 0.8 us
where the time goes in v5:
time: 65.5 us; the launch traced here: 65.4 us
  Pallas kernels  63.9 us (98%)
  local copies, waits for them, and re-layouts  0.8 us (1%)
  between operations  0.72 us (1%)
    pallas_call x1, Pallas kernels, run(): pl.pallas_call(functools.partial(kernel, nz), out_shape=(jax.ShapeDtypeSt...  63.9 us

profile of v5, /device:TPU:1, one launch (start us, length us, event | category | flops | bytes accessed | tf_op | source)
XLA Modules:
  0.0 65.4 jit_solution(7684759350237804776)
XLA Ops:
  0.0 0.0 copy-start
  0.0 63.9 %shard_map.30 = (f32[16,8192]{1,0:T(8,128)S(1)}, s32[1]{0:T(128)}, s32[2,256]{1,0:T(2,128)S(1)}) custom-call(s32[1]{0:T(128)} %constant.14.clone.1.turn, s32[2,256]{1,0:T(2,128)} %bitcast.7, bf16[2,256,512]{2,1,0:T(8,128)(2,1)} %factors.1), custom_call_target="tpu_custom_call" | custom-call | tf_op jit(solution)/shard_map/pallas_call | solution.py:469
  64.6 0.0 copy-done
  64.6 0.8 %copy.22 = f32[16,8192]{1,0:T(8,128)} copy(f32[16,8192]{1,0:T(8,128)S(1)} %get-tuple-element.53) | data formatting | bytes 1048576
  (1 shorter events, 0.0 us)
Async XLA Ops:
  0.0 64.6 %copy-start = (bf16[2,256,512]{2,1,0:T(8,128)(2,1)S(1)}, bf16[2,256,512]{2,1,0:T(8,128)(2,1)}, u32[]{:S(2)}) copy-start(bf16[2,256,512]{2,1,0:T(8,128)(2,1)} %factors.1) | copy-start | bytes 1572868

commit v6 on v5

--- a/solution.py
+++ b/solution.py
@@ -18,7 +18,7 @@
 STEP = 16.0
 TOP = 32000.0
 ROUTES = ("skip", 0), ("skip", 1)
-STEPS = (0, (6, 3)), (1, (6, 3)), (0, (4, 1)), (1, (4, 1)), (0, (2,)), (1, (2,))
+STEPS = (0, (6, 3)), (1, (6,)), (0, (4,)), (1, (3,)), (0, (1,)), (1, (4, 1)), (0, (2,)), (1, (2,))
 FIRST = (8, 7, 5), (8, 7, 5)
 BALANCE, FIXES = 4, 6
 

time: 65.5 us -> 65.4 us (level)
  no operation moved by 1% of the time
where the time goes in v6:
time: 65.4 us; the launch traced here: 65.3 us
  Pallas kernels  63.7 us (97%)
  local copies, waits for them, and re-layouts  0.8 us (1%)
  between operations  0.72 us (1%)
    pallas_call x1, Pallas kernels, run(): pl.pallas_call(functools.partial(kernel, nz), out_shape=(jax.ShapeDtypeSt...  63.7 us

profile of v6, /device:TPU:1, one launch (start us, length us, event | category | flops | bytes accessed | tf_op | source)
XLA Modules:
  0.0 65.3 jit_solution(1935454128655575348)
XLA Ops:
  0.0 0.0 copy-start
  0.0 63.7 %shard_map.30 = (f32[16,8192]{1,0:T(8,128)S(1)}, s32[1]{0:T(128)}, s32[2,256]{1,0:T(2,128)S(1)}) custom-call(s32[1]{0:T(128)} %constant.14.clone.1.turn, s32[2,256]{1,0:T(2,128)} %bitcast.7, bf16[2,256,512]{2,1,0:T(8,128)(2,1)} %factors.1), custom_call_target="tpu_custom_call" | custom-call | tf_op jit(solution)/shard_map/pallas_call | solution.py:469
  64.4 0.0 copy-done
  64.5 0.8 %copy.22 = f32[16,8192]{1,0:T(8,128)} copy(f32[16,8192]{1,0:T(8,128)S(1)} %get-tuple-element.53) | data formatting | bytes 1048576
  (1 shorter events, 0.0 us)
Async XLA Ops:
  0.0 64.4 %copy-start = (bf16[2,256,512]{2,1,0:T(8,128)(2,1)S(1)}, bf16[2,256,512]{2,1,0:T(8,128)(2,1)}, u32[]{:S(2)}) copy-start(bf16[2,256,512]{2,1,0:T(8,128)(2,1)} %factors.1) | copy-start | bytes 1572868
